TPU v7x, 32 devices: a whole 2x2x4 slice. The times are simulated.
32 devices in a mesh: run: 4 (over z), feat: 2 (over core), vox: 4 (over y, x).
Axes of the slice: x: 2, y: 2, z: 4, core: 2. Of those that a mesh axis runs over, the one named last changes fastest.
Arguments:
- stimulus: bfloat16 [4, 512, 256], P('run', None, 'feat')
- responses: bfloat16 [4, 512, 512], P('run', None, 'vox')
- run_lengths: int32 [4], P('run'), may hold values from 1 to 512, 1536 in all
- lag_steps: int32 [4], replicated, may hold values from 0 to 7, as said below
- ridge_grid: float32 [16], replicated, may hold values from 0.05 to 5
- ridge_pick: int32 [4, 2], P('run'), may hold values from 0 to 15
Outputs:
- weights: float32 [4, 2, 1024, 512], P('run', None, 'feat', 'vox')
- fold_errors: float32 [4, 2, 512], P('run', None, 'vox')
Inputs may be any that keep to these rules, and one draw needn't show every extreme that they name: lag_steps[j] is 2 j or 2 j + 1; lag_steps[0] is 0 and the last entry is 7.
All inputs are finite; a program needn't handle non-finite values. No bound on the sum of `run_lengths` on one device may be relied on, other than what follows from the above.
Results may differ from a plain program's by a relative error of at most 0.0003.
Values may be sent and summed in bfloat16 or wider, within the bound.
A program may use at most 128 MiB of HBM per device.

v0:
```python
import jax
import jax.numpy as jnp
from jax import lax
from jax.sharding import PartitionSpec as P


def carried_in(part, axis, combine, identity, reverse):
    count = lax.axis_size(axis)
    place = lax.axis_index(axis)
    ahead = count - 1 - place if reverse else place
    gathered = jax.tree.map(lambda a: lax.all_gather(a, axis), part)
    state = jax.tree.map(lambda a, e: jnp.zeros_like(a) + jnp.asarray(e, a.dtype), part, identity)

    def one(hop, state):
        source = count - 1 - hop if reverse else hop
        return combine(
            state, jax.tree.map(lambda a: lax.dynamic_index_in_dim(a, source, 0, False), gathered)
        )

    return lax.fori_loop(0, ahead, one, state)


def build_features(stim_run, lag_steps, length):
    count_t = stim_run.shape[0]
    steps_t = jnp.arange(count_t, dtype=jnp.int32)
    pieces = []
    for j in range(lag_steps.shape[0]):
        lag = lag_steps[j]
        shifted = jnp.roll(stim_run, lag, axis=0)
        keep = (steps_t >= lag) & (steps_t < length)
        pieces.append(jnp.where(keep[:, None], shifted, jnp.zeros_like(shifted)))
    stacked = jnp.stack(pieces, axis=2)
    return stacked.reshape(count_t, stim_run.shape[1] * lag_steps.shape[0])


def add_terms(first, second):
    return tuple((left + right for left, right in zip(first, second)))


def solve_fold(full_gram, full_cross, count, penalty, feats, masked, length):
    width = full_gram.shape[0]
    eye = jnp.eye(width, dtype=jnp.float32)
    cross_s = full_cross / count
    feats_wide = feats.astype(jnp.float32)
    target_wide = masked.astype(jnp.float32)

    def one_penalty(value):
        system = full_gram / count + value * eye
        lower = jnp.linalg.cholesky(system)
        inner = lax.linalg.triangular_solve(
            lower, cross_s, left_side=True, lower=True, transpose_a=False
        )
        solved = lax.linalg.triangular_solve(
            lower, inner, left_side=True, lower=True, transpose_a=True
        )
        predicted = jnp.dot(feats_wide, solved, precision=lax.Precision.HIGHEST)
        errors = jnp.sum((target_wide - predicted) ** 2, axis=0) / length.astype(jnp.float32)
        return (solved, errors)

    return lax.map(one_penalty, penalty)


def look_up(picks, ridge_grid):
    table_ids = jnp.arange(ridge_grid.shape[0], dtype=jnp.int32)
    hits = picks[:, None] == table_ids[None, :]
    return jnp.sum(
        jnp.where(hits, ridge_grid[None, :], jnp.zeros_like(ridge_grid)[None, :]), axis=1
    )


def local(stimulus, responses, run_lengths, lag_steps, ridge_grid, ridge_pick):
    whole = lax.all_gather(stimulus, "feat", axis=2, tiled=True)
    length = run_lengths[0]
    feats = build_features(whole[0], lag_steps, length)
    count_feat = lax.axis_size("feat")
    count_vox = lax.axis_size("vox")
    width = feats.shape[1]
    half = width // count_feat
    quarter = width // count_vox
    own_rows = lax.dynamic_slice_in_dim(feats, lax.axis_index("feat") * half, half, 1)
    columns = lax.dynamic_slice_in_dim(feats, lax.axis_index("vox") * quarter, quarter, 1)
    steps_t = jnp.arange(feats.shape[0], dtype=jnp.int32)
    masked = jnp.where((steps_t < length)[:, None], responses[0], jnp.zeros_like(responses[0]))
    contract = (((0,), (0,)), ((), ()))
    gram = lax.dot_general(own_rows, columns, contract, preferred_element_type=jnp.float32)
    cross = lax.dot_general(own_rows, masked, contract, preferred_element_type=jnp.float32)
    count = length.astype(jnp.float32).reshape(1)
    zeros = (jnp.zeros_like(gram), jnp.zeros_like(cross), jnp.zeros_like(count))
    before = carried_in((gram, cross, count), "run", add_terms, zeros, False)
    after = carried_in((gram, cross, count), "run", add_terms, zeros, True)
    rest_gram, rest_cross, rest_count = add_terms(before, after)
    wide_rows = lax.all_gather(rest_gram, "vox", axis=1, tiled=True)
    full_gram, full_cross = (
        lax.all_gather(wide_rows, "feat", axis=0, tiled=True),
        lax.all_gather(rest_cross, "feat", axis=0, tiled=True),
    )
    picks = ridge_pick[0]
    solved, errors = solve_fold(
        full_gram, full_cross, rest_count[0], look_up(picks, ridge_grid), feats, masked, length
    )
    kept = lax.dynamic_slice_in_dim(solved, lax.axis_index("feat") * half, half, 1)
    return (kept[None], errors[None])


def solution(mesh):
    return jax.shard_map(
        local,
        mesh=mesh,
        in_specs=(
            P("run", None, "feat"),
            P("run", None, "vox"),
            P("run"),
            P(),
            P(),
            P("run", None),
        ),
        out_specs=(P("run", None, "feat", "vox"), P("run", None, "vox")),
        check_vma=False,
    )
```

profile of v0, /device:TPU:0, one launch (start us, length us, event | category | flops | bytes accessed | tf_op | source)
XLA Modules:
  0.0 881.4 jit_solution(4735311009072833869)
XLA Ops:
  29.7 13.4 %all-reduce.1 = f32[4]{0:T(128)S(1)} all-reduce(f32[4]{0:T(128)S(1)} %dynamic-update-slice.75), channel_id=1, replica_groups=mesh['run'=4,'feat'=2,'vox'=4] {'run'}, use_global_device_ids=true, to_apply=%add.1 | all-reduce | flops 4 | bytes 32
  43.1 14.8 %all-gather.13.cloned.1.call-done = f32[2048,128]{1,0:T(8,128)} async-done(((f32[512,128]{1,0:T(8,128)}), f32[2048,128]{1,0:T(8,128)}) %all-gather.13.cloned.1.call-update) | async-done | bytes 1048592 | tf_op jit(solution)/shard_map/all_gather | solution.py:11
  57.9 47.5 %all-gather.11.cloned.1.call-done = f32[2048,256]{1,0:T(8,128)} async-done(((f32[512,256]{1,0:T(8,128)}), f32[2048,256]{1,0:T(8,128)}) %all-gather.11.cloned.1.call-update) | async-done | bytes 2097168 | tf_op jit(solution)/shard_map/all_gather | solution.py:11
  105.5 10.3 %while.49 = (s32[]{:T(128)}, f32[512,256]{1,0:T(8,128)S(1)}, f32[512,128]{1,0:T(8,128)S(1)}, f32[1]{0:T(128)}, s32[]{:T(128)}, /*index=5*/f32[4,512,256]{2,1,0:T...) while((s32[]{:T(128)}, f32[512,256]{1,0:T(8,128)S(1)}, ...), condition=%wide.region_4.6_spmd, body=%wide.region_3.5_spmd.sunk | while | flops 196615 | bytes 2359491 | solution.py:20
  117.3 34.1 %all-gather.7.cloned.1.call-done = f32[512,1024]{0,1:T(8,128)} async-done(((f32[512,256]{0,1:T(8,128)}), f32[512,1024]{0,1:T(8,128)}) %all-gather.7.cloned.1.call-update) | async-done | bytes 2097168 | tf_op jit(solution)/shard_map/all_gather | solution.py:92
  155.5 11.1 %all-gather.9.cloned.1.call-done = f32[1024,1024]{0,1:T(8,128)} async-done(((f32[512,1024]{0,1:T(8,128)}), f32[1024,1024]{0,1:T(8,128)}) %all-gather.9.cloned.1.call-update) | async-done | bytes 4194320 | tf_op jit(solution)/shard_map/all_gather | solution.py:94
  166.5 706.2 %while.51 = (s32[]{:T(128)}, f32[2,1024,128]{2,1,0:T(8,128)}, f32[2,128]{1,0:T(2,128)S(1)}, f32[]{:T(128)}, f32[1024,1024]{0,1:T(8,128)}, /*index=5*/f32[2]{0:T(...) while((s32[]{:T(128)}, f32[2,1024,128]{2,1,0:T(8,128)}, ...), condition=%wide.region_23.25_spmd.clone, body=%wide.region_5.24_spmd.clone.sunk | while | flops 5452662272 | bytes 122106424 | solution.py:60
  185.5 11.7 %cholesky.1066 = f32[128,128]{1,0:T(8,128)S(1)} custom-call(f32[128,128]{1,0:T(8,128)S(1)} %cholesky.1065), custom_call_target="Cholesky" | custom-call | tf_op jit(solution)/shard_map/while/body/eval_jaxpr/jit(cholesky)/cholesky | solution.py:49
  197.2 9.8 %custom-call.140 = f32[1,128,128]{1,2,0:T(8,128)S(1)} custom-call(f32[1,128,128]{2,1,0:T(8,128)S(1)} %get-tuple-element.722), custom_call_target="InvertDiagBlocksLowerTriangular" | custom-call | tf_op jit(solution)/shard_map/while/body/eval_jaxpr/jit(cholesky)/cholesky | solution.py:49
  213.5 12.3 %cholesky.1069 = f32[128,128]{1,0:T(8,128)S(1)} custom-call(f32[128,128]{1,0:T(8,128)S(1)} %cholesky.1068), custom_call_target="Cholesky" | custom-call | tf_op jit(solution)/shard_map/while/body/eval_jaxpr/jit(cholesky)/cholesky | solution.py:49
  228.2 9.8 %custom-call.141 = f32[1,128,128]{1,2,0:T(8,128)S(1)} custom-call(f32[1,128,128]{2,1,0:T(8,128)S(1)} %get-tuple-element.726), custom_call_target="InvertDiagBlocksLowerTriangular" | custom-call | tf_op jit(solution)/shard_map/while/body/eval_jaxpr/jit(cholesky)/cholesky | solution.py:49
  241.4 11.7 %cholesky.1071 = f32[128,128]{1,0:T(8,128)S(1)} custom-call(f32[128,128]{1,0:T(8,128)S(1)} %cholesky.1070), custom_call_target="Cholesky" | custom-call | tf_op jit(solution)/shard_map/while/body/eval_jaxpr/jit(cholesky)/cholesky | solution.py:49
  268.4 11.9 %cholesky.1073 = f32[128,128]{1,0:T(8,128)S(1)} custom-call(f32[128,128]{1,0:T(8,128)S(1)} %cholesky.1072), custom_call_target="Cholesky" | custom-call | tf_op jit(solution)/shard_map/while/body/eval_jaxpr/jit(cholesky)/cholesky | solution.py:49
  295.5 11.7 %cholesky.1075 = f32[128,128]{1,0:T(8,128)S(1)} custom-call(f32[128,128]{1,0:T(8,128)S(1)} %cholesky.1074), custom_call_target="Cholesky" | custom-call | tf_op jit(solution)/shard_map/while/body/eval_jaxpr/jit(cholesky)/cholesky | solution.py:49
  309.2 10.0 %custom-call.144 = f32[1,128,128]{1,2,0:T(8,128)S(1)} custom-call(f32[1,128,128]{2,1,0:T(8,128)S(1)} %get-tuple-element.732), custom_call_target="InvertDiagBlocksLowerTriangular" | custom-call | tf_op jit(solution)/shard_map/while/body/eval_jaxpr/jit(cholesky)/cholesky | solution.py:49
  322.5 11.7 %cholesky.1077 = f32[128,128]{1,0:T(8,128)S(1)} custom-call(f32[128,128]{1,0:T(8,128)S(1)} %cholesky.1076), custom_call_target="Cholesky" | custom-call | tf_op jit(solution)/shard_map/while/body/eval_jaxpr/jit(cholesky)/cholesky | solution.py:49
  348.9 12.1 %cholesky.1079 = f32[128,128]{1,0:T(8,128)S(1)} custom-call(f32[128,128]{1,0:T(8,128)S(1)} %cholesky.1078), custom_call_target="Cholesky" | custom-call | tf_op jit(solution)/shard_map/while/body/eval_jaxpr/jit(cholesky)/cholesky | solution.py:49
  375.4 11.7 %cholesky.1080 = f32[128,128]{1,0:T(8,128)S(1)} custom-call(f32[128,128]{1,0:T(8,128)S(1)} %convolution_subtract_fusion.48), custom_call_target="Cholesky" | custom-call | tf_op jit(solution)/shard_map/while/body/eval_jaxpr/jit(cholesky)/cholesky | solution.py:49
  393.9 27.4 %while.52 = (s32[]{:T(128)}, f32[1024,1024]{1,0:T(8,128)}, s32[8,2]{0,1:T(2,128)S(1)}, f32[8,128,128]{2,1,0:T(8,128)}, s32[]{:T(128)}) while((s32[]{:T(128)}, f32[1024,1024]{1,0:T(8,128)}, s32[8,2]{0,1:T(2,128)S(1)}, f32[8,128,128]{2,1,0:T(8,128)}, s32[]{:T(128)}) %tuple.173), condition=%wide.while_cond, body=%wide.while_body.sunk | while | flops 2 | bytes 132705 | solution.py:53
  421.3 79.6 %custom-call.148 = f32[8,128,128]{1,2,0:T(8,128)S(1)} custom-call(f32[8,128,128]{2,1,0:T(8,128)} %get-tuple-element.748), custom_call_target="InvertDiagBlocksLowerTriangular" | custom-call | tf_op jit(solution)/shard_map/while/body/eval_jaxpr/triangular_solve | solution.py:53
  538.2 11.7 %cholesky.1066 = f32[128,128]{1,0:T(8,128)S(1)} custom-call(f32[128,128]{1,0:T(8,128)S(1)} %cholesky.1065), custom_call_target="Cholesky" | custom-call | tf_op jit(solution)/shard_map/while/body/eval_jaxpr/jit(cholesky)/cholesky | solution.py:49
  549.9 9.8 %custom-call.140 = f32[1,128,128]{1,2,0:T(8,128)S(1)} custom-call(f32[1,128,128]{2,1,0:T(8,128)S(1)} %get-tuple-element.722), custom_call_target="InvertDiagBlocksLowerTriangular" | custom-call | tf_op jit(solution)/shard_map/while/body/eval_jaxpr/jit(cholesky)/cholesky | solution.py:49
  566.2 11.9 %cholesky.1069 = f32[128,128]{1,0:T(8,128)S(1)} custom-call(f32[128,128]{1,0:T(8,128)S(1)} %cholesky.1068), custom_call_target="Cholesky" | custom-call | tf_op jit(solution)/shard_map/while/body/eval_jaxpr/jit(cholesky)/cholesky | solution.py:49
  593.7 11.7 %cholesky.1071 = f32[128,128]{1,0:T(8,128)S(1)} custom-call(f32[128,128]{1,0:T(8,128)S(1)} %cholesky.1070), custom_call_target="Cholesky" | custom-call | tf_op jit(solution)/shard_map/while/body/eval_jaxpr/jit(cholesky)/cholesky | solution.py:49
  620.7 11.9 %cholesky.1073 = f32[128,128]{1,0:T(8,128)S(1)} custom-call(f32[128,128]{1,0:T(8,128)S(1)} %cholesky.1072), custom_call_target="Cholesky" | custom-call | tf_op jit(solution)/shard_map/while/body/eval_jaxpr/jit(cholesky)/cholesky | solution.py:49
  647.8 11.7 %cholesky.1075 = f32[128,128]{1,0:T(8,128)S(1)} custom-call(f32[128,128]{1,0:T(8,128)S(1)} %cholesky.1074), custom_call_target="Cholesky" | custom-call | tf_op jit(solution)/shard_map/while/body/eval_jaxpr/jit(cholesky)/cholesky | solution.py:49
  661.5 10.2 %custom-call.144 = f32[1,128,128]{1,2,0:T(8,128)S(1)} custom-call(f32[1,128,128]{2,1,0:T(8,128)S(1)} %get-tuple-element.732), custom_call_target="InvertDiagBlocksLowerTriangular" | custom-call | tf_op jit(solution)/shard_map/while/body/eval_jaxpr/jit(cholesky)/cholesky | solution.py:49
  675.0 11.7 %cholesky.1077 = f32[128,128]{1,0:T(8,128)S(1)} custom-call(f32[128,128]{1,0:T(8,128)S(1)} %cholesky.1076), custom_call_target="Cholesky" | custom-call | tf_op jit(solution)/shard_map/while/body/eval_jaxpr/jit(cholesky)/cholesky | solution.py:49
  701.4 11.9 %cholesky.1079 = f32[128,128]{1,0:T(8,128)S(1)} custom-call(f32[128,128]{1,0:T(8,128)S(1)} %cholesky.1078), custom_call_target="Cholesky" | custom-call | tf_op jit(solution)/shard_map/while/body/eval_jaxpr/jit(cholesky)/cholesky | solution.py:49
  727.7 11.7 %cholesky.1080 = f32[128,128]{1,0:T(8,128)S(1)} custom-call(f32[128,128]{1,0:T(8,128)S(1)} %convolution_subtract_fusion.48), custom_call_target="Cholesky" | custom-call | tf_op jit(solution)/shard_map/while/body/eval_jaxpr/jit(cholesky)/cholesky | solution.py:49
  746.2 27.4 %while.52 = (s32[]{:T(128)}, f32[1024,1024]{1,0:T(8,128)}, s32[8,2]{0,1:T(2,128)S(1)}, f32[8,128,128]{2,1,0:T(8,128)}, s32[]{:T(128)}) while((s32[]{:T(128)}, f32[1024,1024]{1,0:T(8,128)}, s32[8,2]{0,1:T(2,128)S(1)}, f32[8,128,128]{2,1,0:T(8,128)}, s32[]{:T(128)}) %tuple.173), condition=%wide.while_cond, body=%wide.while_body.sunk | while | flops 2 | bytes 132705 | solution.py:53
  773.6 79.6 %custom-call.148 = f32[8,128,128]{1,2,0:T(8,128)S(1)} custom-call(f32[8,128,128]{2,1,0:T(8,128)} %get-tuple-element.748), custom_call_target="InvertDiagBlocksLowerTriangular" | custom-call | tf_op jit(solution)/shard_map/while/body/eval_jaxpr/triangular_solve | solution.py:53
  (336 shorter events, 324.6 us)
Async XLA Ops:
  7.2 18.7 %copy-start.5 = (bf16[1,512,128]{2,1,0:T(8,128)(2,1)S(1)}, bf16[1,512,128]{2,1,0:T(8,128)(2,1)}, u32[]{:S(2)}) copy-start(bf16[1,512,128]{2,1,0:T(8,128)(2,1)} %param.15) | copy-start | bytes 393220
  7.2 50.7 %all-gather.13.cloned.1.call-start = ((), (), s32[]{:S(2)}) async-start(), calls=%async_computation.3 | async-start | bytes 1310720 | tf_op jit(solution)/shard_map/all_gather | solution.py:11
  24.5 3.8 copy-start.9
  25.8 79.6 %copy-start.2 = (bf16[512,1024]{0,1:T(8,128)(2,1)}, bf16[512,1024]{0,1:T(8,128)(2,1)S(1)}, u32[]{:S(2)}) copy-start(bf16[512,1024]{0,1:T(8,128)(2,1)S(1)} %reshape.193) | copy-start | bytes 3145732
  27.1 78.3 %all-gather.11.cloned.1.call-start = ((), (), s32[]{:S(2)}) async-start(), calls=%async_computation.2 | async-start | bytes 2621440 | tf_op jit(solution)/shard_map/all_gather | solution.py:11
  28.3 123.2 %all-gather.7.cloned.1.call-start = ((), (), s32[]{:S(2)}) async-start(), calls=%async_computation | async-start | bytes 2621440 | tf_op jit(solution)/shard_map/all_gather | solution.py:92
  116.1 36.9 %copy-start.7 = (f32[16]{0:T(128)S(1)}, f32[16]{0:T(128)}, u32[]{:S(2)}) copy-start(f32[16]{0:T(128)} %param.18) | copy-start | bytes 196
  116.1 36.9 %copy-start.8 = (s32[1,2]{1,0:T(1,128)S(1)}, s32[1,2]{1,0:T(1,128)}, u32[]{:S(2)}) copy-start(s32[1,2]{1,0:T(1,128)} %param.19) | copy-start | bytes 28
  117.2 49.3 %all-gather.9.cloned.1.call-start = ((), (), s32[]{:S(2)}) async-start(), calls=%async_computation.1 | async-start | bytes 6291456 | tf_op jit(solution)/shard_map/all_gather | solution.py:94
  183.5 2.0 copy-start.1
  500.9 8.2 copy-start
  511.8 5.2 copy-start.3
  517.1 2.0 copy-start.4
  536.2 2.0 copy-start.1
  853.2 8.2 copy-start
  864.2 5.2 copy-start.3
  869.4 2.0 copy-start.4
  872.7 1.9 copy-start.6
Sparse Core Ops, SparseCore 0:
  27.2 30.6 all-gather.12
  60.0 45.3 all-gather.10
  117.4 34.0 all-gather.6
  152.8 13.6 all-gather.8
where the time goes:
time: 888 us; the launch traced here: 881 us
  other arithmetic  548 us (62%)
  waiting for transfers between devices  108 us (12%)
  local copies, waits for them, and re-layouts  86 us (10%)
  matrix products  83.5 us (9%)
  between operations  22.6 us (3%)
  blocking collectives  17.9 us (2%)
  loops' own time  15.6 us (2%)
    another operation x60, other arithmetic, one_penalty(): lower = jnp.linalg.cholesky(system)  345 us
    another operation x6, other arithmetic, one_penalty(): lax.linalg.triangular_solve(lower, inner, left_side=True, lower=True, tra...  169 us
    all_gather x2, waiting for transfers between devices, carried_in(): gathered = jax.tree.map(lambda a: lax.all_gather(a, axis), part)  62.3 us
    another operation x48, local copies, waits for them, and re-layouts  54.7 us
    another operation x28, matrix products, one_penalty(): lower = jnp.linalg.cholesky(system)  46.2 us
    all_gather x1, waiting for transfers between devices, local(): wide_rows = lax.all_gather(rest_gram, 'vox', axis=1, tiled=True)  34.1 us
    another operation x30, matrix products, one_penalty(): lax.linalg.triangular_solve(lower, cross_s, left_side=True, lower=True, t...  19.5 us
  transfers between devices with their start and end apart: 4, of which 4 were waited for; matrix products, arithmetic and copies ran while one was open for 0% of the time, Pallas kernels for 0%

commit v1 on v0

--- a/solution.py
+++ b/solution.py
@@ -2,6 +2,12 @@
 import jax.numpy as jnp
 from jax import lax
 from jax.sharding import PartitionSpec as P
+
+
+def in_order(blocks, dim):
+    dims = list(blocks.shape[1:])
+    dims[dim] *= blocks.shape[0]
+    return jnp.moveaxis(blocks, 0, dim).reshape(dims)
 
 
 def carried_in(part, axis, combine, identity, reverse):
@@ -89,7 +95,19 @@
     before = carried_in((gram, cross, count), "run", add_terms, zeros, False)
     after = carried_in((gram, cross, count), "run", add_terms, zeros, True)
     rest_gram, rest_cross, rest_count = add_terms(before, after)
-    wide_rows = lax.all_gather(rest_gram, "vox", axis=1, tiled=True)
+    count_2 = lax.axis_size("vox")
+    pairs = [(i, (i + 1) % count_2) for i in range(count_2)]
+    back = [(b, a_2) for a_2, b in pairs]
+    lower_2, upper = ([], [])
+    for step in range(count_2 - 1):
+        if step % 2 == 0:
+            lower_2.append(lax.ppermute(lower_2[-1] if lower_2 else rest_gram, "vox", pairs))
+        else:
+            upper.append(lax.ppermute(upper[-1] if upper else rest_gram, "vox", back))
+    blocks = jnp.stack([*lower_2[::-1], rest_gram, *upper])
+    shift = lax.axis_index("vox") - len(lower_2)
+    blocks = blocks[(jnp.arange(count_2) - shift) % count_2]
+    wide_rows = in_order(blocks, 1)
     full_gram, full_cross = (
         lax.all_gather(wide_rows, "feat", axis=0, tiled=True),
         lax.all_gather(rest_cross, "feat", axis=0, tiled=True),

time: 888 us -> 894 us (level)
    all_gather x1 -> x0, waiting for transfers between devices: 34.1 us -> none  [local(): wide_rows = lax.all_gather(rest_gram, 'vox', axis=1, tiled=True)]
    ppermute x0 -> x3, waiting for transfers between devices: none -> 33.5 us  [the longest x2 22.9 us: local(): lax.ppermute(lower_2[-1] if lower_2 else rest_gram, 'vox', pairs)]
  transfers between devices with their start and end apart: 4 -> 6, of which waited for: 4 -> 6; matrix products, arithmetic and copies ran while one was open for 0% -> 0% of each run, Pallas kernels for 0% -> 0%
where the time goes in v1:
time: 894 us; the launch traced here: 887 us
  other arithmetic  549 us (61%)
  waiting for transfers between devices  104 us (12%)
  local copies, waits for them, and re-layouts  91.4 us (10%)
  matrix products  83.4 us (9%)
  between operations  22.5 us (3%)
  blocking collectives  17.9 us (2%)
  loops' own time  15.6 us (2%)
    another operation x60, other arithmetic, one_penalty(): lower = jnp.linalg.cholesky(system)  345 us
    another operation x6, other arithmetic, one_penalty(): lax.linalg.triangular_solve(lower, inner, left_side=True, lower=True, tra...  169 us
    all_gather x2, waiting for transfers between devices, carried_in(): gathered = jax.tree.map(lambda a: lax.all_gather(a, axis), part)  62.3 us
    another operation x48, local copies, waits for them, and re-layouts  54.7 us
    another operation x28, matrix products, one_penalty(): lower = jnp.linalg.cholesky(system)  46.2 us
    ppermute x2, waiting for transfers between devices, local(): lax.ppermute(lower_2[-1] if lower_2 else rest_gram, 'vox', pairs)  22.9 us
    another operation x30, matrix products, one_penalty(): lax.linalg.triangular_solve(lower, cross_s, left_side=True, lower=True, t...  19.5 us
  transfers between devices with their start and end apart: 6, of which 6 were waited for; matrix products, arithmetic and copies ran while one was open for 0% of the time, Pallas kernels for 0%

profile of v1, /device:TPU:0, one launch (start us, length us, event | category | flops | bytes accessed | tf_op | source)
XLA Modules:
  0.0 887.1 jit_solution(1703808115321104832)
XLA Ops:
  29.7 13.4 %all-reduce.1 = f32[4]{0:T(128)S(1)} all-reduce(f32[4]{0:T(128)S(1)} %dynamic-update-slice.75), channel_id=1, replica_groups=mesh['run'=4,'feat'=2,'vox'=4] {'run'}, use_global_device_ids=true, to_apply=%add.1 | all-reduce | flops 4 | bytes 32
  43.1 14.8 %all-gather.10.cloned.1.call-done = f32[2048,128]{1,0:T(8,128)} async-done(((f32[512,128]{1,0:T(8,128)}), f32[2048,128]{1,0:T(8,128)}) %all-gather.10.cloned.1.call-update) | async-done | bytes 1048592 | tf_op jit(solution)/shard_map/all_gather | solution.py:17
  57.9 47.5 %all-gather.8.cloned.1.call-done = f32[2048,256]{1,0:T(8,128)} async-done(((f32[512,256]{1,0:T(8,128)}), f32[2048,256]{1,0:T(8,128)}) %all-gather.8.cloned.1.call-update) | async-done | bytes 2097168 | tf_op jit(solution)/shard_map/all_gather | solution.py:17
  105.5 10.3 %while.49 = (s32[]{:T(128)}, f32[512,256]{1,0:T(8,128)S(1)}, f32[512,128]{1,0:T(8,128)S(1)}, f32[1]{0:T(128)}, s32[]{:T(128)}, /*index=5*/f32[4,512,256]{2,1,0:T...) while((s32[]{:T(128)}, f32[512,256]{1,0:T(8,128)S(1)}, ...), condition=%wide.region_4.6_spmd, body=%wide.region_3.5_spmd.sunk | while | flops 196615 | bytes 2359491 | solution.py:26
  119.0 12.8 %collective-permute-done = f32[512,256]{1,0:T(8,128)S(1)} collective-permute-done((f32[512,256]{1,0:T(8,128)S(1)}, f32[512,256]{1,0:T(8,128)S(1)}, u32[]{:S(2)}, u32[]{:S(2)}) %collective-permute-start) | collective-permute-done | bytes 524320 | tf_op jit(solution)/shard_map/ppermute | solution.py:104
  132.3 10.6 %collective-permute-done.2 = f32[512,256]{1,0:T(8,128)S(1)} collective-permute-done((f32[512,256]{1,0:T(8,128)S(1)}, f32[512,256]{1,0:T(8,128)S(1)}, u32[]{:S(2)}, u32[]{:S(2)}) %collective-permute-start.2) | collective-permute-done | bytes 524320 | tf_op jit(solution)/shard_map/ppermute | solution.py:106
  143.0 10.1 %collective-permute-done.1 = f32[512,256]{1,0:T(8,128)S(1)} collective-permute-done((f32[512,256]{1,0:T(8,128)S(1)}, f32[512,256]{1,0:T(8,128)S(1)}, u32[]{:S(2)}, u32[]{:S(2)}) %collective-permute-start.1) | collective-permute-done | bytes 524320 | tf_op jit(solution)/shard_map/ppermute | solution.py:104
  172.3 706.2 %while.51 = (s32[]{:T(128)}, f32[2,1024,128]{2,1,0:T(8,128)}, f32[2,128]{1,0:T(2,128)S(1)}, f32[]{:T(128)}, f32[1024,1024]{0,1:T(8,128)}, /*index=5*/f32[2]{0:T(...) while((s32[]{:T(128)}, f32[2,1024,128]{2,1,0:T(8,128)}, ...), condition=%wide.region_23.25_spmd.clone, body=%wide.region_5.0_spmd.clone.sunk | while | flops 5452662272 | bytes 122106424 | solution.py:66
  191.3 11.7 %cholesky.1066 = f32[128,128]{1,0:T(8,128)S(1)} custom-call(f32[128,128]{1,0:T(8,128)S(1)} %cholesky.1065), custom_call_target="Cholesky" | custom-call | tf_op jit(solution)/shard_map/while/body/eval_jaxpr/jit(cholesky)/cholesky | solution.py:55
  203.0 9.8 %custom-call.142 = f32[1,128,128]{1,2,0:T(8,128)S(1)} custom-call(f32[1,128,128]{2,1,0:T(8,128)S(1)} %get-tuple-element.722), custom_call_target="InvertDiagBlocksLowerTriangular" | custom-call | tf_op jit(solution)/shard_map/while/body/eval_jaxpr/jit(cholesky)/cholesky | solution.py:55
  219.2 12.3 %cholesky.1069 = f32[128,128]{1,0:T(8,128)S(1)} custom-call(f32[128,128]{1,0:T(8,128)S(1)} %cholesky.1068), custom_call_target="Cholesky" | custom-call | tf_op jit(solution)/shard_map/while/body/eval_jaxpr/jit(cholesky)/cholesky | solution.py:55
  247.2 11.7 %cholesky.1071 = f32[128,128]{1,0:T(8,128)S(1)} custom-call(f32[128,128]{1,0:T(8,128)S(1)} %cholesky.1070), custom_call_target="Cholesky" | custom-call | tf_op jit(solution)/shard_map/while/body/eval_jaxpr/jit(cholesky)/cholesky | solution.py:55
  274.2 11.9 %cholesky.1073 = f32[128,128]{1,0:T(8,128)S(1)} custom-call(f32[128,128]{1,0:T(8,128)S(1)} %cholesky.1072), custom_call_target="Cholesky" | custom-call | tf_op jit(solution)/shard_map/while/body/eval_jaxpr/jit(cholesky)/cholesky | solution.py:55
  301.3 11.7 %cholesky.1075 = f32[128,128]{1,0:T(8,128)S(1)} custom-call(f32[128,128]{1,0:T(8,128)S(1)} %cholesky.1074), custom_call_target="Cholesky" | custom-call | tf_op jit(solution)/shard_map/while/body/eval_jaxpr/jit(cholesky)/cholesky | solution.py:55
  315.0 10.0 %custom-call.146 = f32[1,128,128]{1,2,0:T(8,128)S(1)} custom-call(f32[1,128,128]{2,1,0:T(8,128)S(1)} %get-tuple-element.732), custom_call_target="InvertDiagBlocksLowerTriangular" | custom-call | tf_op jit(solution)/shard_map/while/body/eval_jaxpr/jit(cholesky)/cholesky | solution.py:55
  328.2 11.7 %cholesky.1077 = f32[128,128]{1,0:T(8,128)S(1)} custom-call(f32[128,128]{1,0:T(8,128)S(1)} %cholesky.1076), custom_call_target="Cholesky" | custom-call | tf_op jit(solution)/shard_map/while/body/eval_jaxpr/jit(cholesky)/cholesky | solution.py:55
  354.7 12.1 %cholesky.1079 = f32[128,128]{1,0:T(8,128)S(1)} custom-call(f32[128,128]{1,0:T(8,128)S(1)} %cholesky.1078), custom_call_target="Cholesky" | custom-call | tf_op jit(solution)/shard_map/while/body/eval_jaxpr/jit(cholesky)/cholesky | solution.py:55
  381.2 11.7 %cholesky.1080 = f32[128,128]{1,0:T(8,128)S(1)} custom-call(f32[128,128]{1,0:T(8,128)S(1)} %convolution_subtract_fusion.48), custom_call_target="Cholesky" | custom-call | tf_op jit(solution)/shard_map/while/body/eval_jaxpr/jit(cholesky)/cholesky | solution.py:55
  399.7 27.4 %while.52 = (s32[]{:T(128)}, f32[1024,1024]{1,0:T(8,128)}, s32[8,2]{0,1:T(2,128)S(1)}, f32[8,128,128]{2,1,0:T(8,128)}, s32[]{:T(128)}) while((s32[]{:T(128)}, f32[1024,1024]{1,0:T(8,128)}, s32[8,2]{0,1:T(2,128)S(1)}, f32[8,128,128]{2,1,0:T(8,128)}, s32[]{:T(128)}) %tuple.173), condition=%wide.while_cond, body=%wide.while_body.sunk | while | flops 2 | bytes 132705 | solution.py:59
  427.1 79.6 %custom-call.150 = f32[8,128,128]{1,2,0:T(8,128)S(1)} custom-call(f32[8,128,128]{2,1,0:T(8,128)} %get-tuple-element.748), custom_call_target="InvertDiagBlocksLowerTriangular" | custom-call | tf_op jit(solution)/shard_map/while/body/eval_jaxpr/triangular_solve | solution.py:59
  544.0 11.7 %cholesky.1066 = f32[128,128]{1,0:T(8,128)S(1)} custom-call(f32[128,128]{1,0:T(8,128)S(1)} %cholesky.1065), custom_call_target="Cholesky" | custom-call | tf_op jit(solution)/shard_map/while/body/eval_jaxpr/jit(cholesky)/cholesky | solution.py:55
  555.7 9.8 %custom-call.142 = f32[1,128,128]{1,2,0:T(8,128)S(1)} custom-call(f32[1,128,128]{2,1,0:T(8,128)S(1)} %get-tuple-element.722), custom_call_target="InvertDiagBlocksLowerTriangular" | custom-call | tf_op jit(solution)/shard_map/while/body/eval_jaxpr/jit(cholesky)/cholesky | solution.py:55
  571.9 11.9 %cholesky.1069 = f32[128,128]{1,0:T(8,128)S(1)} custom-call(f32[128,128]{1,0:T(8,128)S(1)} %cholesky.1068), custom_call_target="Cholesky" | custom-call | tf_op jit(solution)/shard_map/while/body/eval_jaxpr/jit(cholesky)/cholesky | solution.py:55
  599.5 11.7 %cholesky.1071 = f32[128,128]{1,0:T(8,128)S(1)} custom-call(f32[128,128]{1,0:T(8,128)S(1)} %cholesky.1070), custom_call_target="Cholesky" | custom-call | tf_op jit(solution)/shard_map/while/body/eval_jaxpr/jit(cholesky)/cholesky | solution.py:55
  626.5 11.9 %cholesky.1073 = f32[128,128]{1,0:T(8,128)S(1)} custom-call(f32[128,128]{1,0:T(8,128)S(1)} %cholesky.1072), custom_call_target="Cholesky" | custom-call | tf_op jit(solution)/shard_map/while/body/eval_jaxpr/jit(cholesky)/cholesky | solution.py:55
  653.6 11.7 %cholesky.1075 = f32[128,128]{1,0:T(8,128)S(1)} custom-call(f32[128,128]{1,0:T(8,128)S(1)} %cholesky.1074), custom_call_target="Cholesky" | custom-call | tf_op jit(solution)/shard_map/while/body/eval_jaxpr/jit(cholesky)/cholesky | solution.py:55
  667.3 10.2 %custom-call.146 = f32[1,128,128]{1,2,0:T(8,128)S(1)} custom-call(f32[1,128,128]{2,1,0:T(8,128)S(1)} %get-tuple-element.732), custom_call_target="InvertDiagBlocksLowerTriangular" | custom-call | tf_op jit(solution)/shard_map/while/body/eval_jaxpr/jit(cholesky)/cholesky | solution.py:55
  680.8 11.7 %cholesky.1077 = f32[128,128]{1,0:T(8,128)S(1)} custom-call(f32[128,128]{1,0:T(8,128)S(1)} %cholesky.1076), custom_call_target="Cholesky" | custom-call | tf_op jit(solution)/shard_map/while/body/eval_jaxpr/jit(cholesky)/cholesky | solution.py:55
  707.2 11.9 %cholesky.1079 = f32[128,128]{1,0:T(8,128)S(1)} custom-call(f32[128,128]{1,0:T(8,128)S(1)} %cholesky.1078), custom_call_target="Cholesky" | custom-call | tf_op jit(solution)/shard_map/while/body/eval_jaxpr/jit(cholesky)/cholesky | solution.py:55
  733.5 11.7 %cholesky.1080 = f32[128,128]{1,0:T(8,128)S(1)} custom-call(f32[128,128]{1,0:T(8,128)S(1)} %convolution_subtract_fusion.48), custom_call_target="Cholesky" | custom-call | tf_op jit(solution)/shard_map/while/body/eval_jaxpr/jit(cholesky)/cholesky | solution.py:55
  752.0 27.4 %while.52 = (s32[]{:T(128)}, f32[1024,1024]{1,0:T(8,128)}, s32[8,2]{0,1:T(2,128)S(1)}, f32[8,128,128]{2,1,0:T(8,128)}, s32[]{:T(128)}) while((s32[]{:T(128)}, f32[1024,1024]{1,0:T(8,128)}, s32[8,2]{0,1:T(2,128)S(1)}, f32[8,128,128]{2,1,0:T(8,128)}, s32[]{:T(128)}) %tuple.173), condition=%wide.while_cond, body=%wide.while_body.sunk | while | flops 2 | bytes 132705 | solution.py:59
  779.3 79.6 %custom-call.150 = f32[8,128,128]{1,2,0:T(8,128)S(1)} custom-call(f32[8,128,128]{2,1,0:T(8,128)} %get-tuple-element.748), custom_call_target="InvertDiagBlocksLowerTriangular" | custom-call | tf_op jit(solution)/shard_map/while/body/eval_jaxpr/triangular_solve | solution.py:59
  (348 shorter events, 351.9 us)
Async XLA Ops:
  7.2 18.7 %copy-start.8 = (bf16[1,512,128]{2,1,0:T(8,128)(2,1)S(1)}, bf16[1,512,128]{2,1,0:T(8,128)(2,1)}, u32[]{:S(2)}) copy-start(bf16[1,512,128]{2,1,0:T(8,128)(2,1)} %param.15) | copy-start | bytes 393220
  7.2 50.7 %all-gather.10.cloned.1.call-start = ((), (), s32[]{:S(2)}) async-start(), calls=%async_computation.2 | async-start | bytes 1310720 | tf_op jit(solution)/shard_map/all_gather | solution.py:17
  24.5 3.8 copy-start.12
  25.8 79.6 %copy-start.2 = (bf16[512,1024]{0,1:T(8,128)(2,1)}, bf16[512,1024]{0,1:T(8,128)(2,1)S(1)}, u32[]{:S(2)}) copy-start(bf16[512,1024]{0,1:T(8,128)(2,1)S(1)} %reshape.245) | copy-start | bytes 3145732
  27.1 78.3 %all-gather.8.cloned.1.call-start = ((), (), s32[]{:S(2)}) async-start(), calls=%async_computation.1 | async-start | bytes 2621440 | tf_op jit(solution)/shard_map/all_gather | solution.py:17
  28.3 144.1 %all-gather.6.cloned.1.call-start = ((), (), s32[]{:S(2)}) async-start(), calls=%async_computation | async-start | bytes 6291456 | tf_op jit(solution)/shard_map/all_gather | solution.py:112
  116.0 15.8 %collective-permute-start = (f32[512,256]{1,0:T(8,128)S(1)}, f32[512,256]{1,0:T(8,128)S(1)}, u32[]{:S(2)}, u32[]{:S(2)}) collective-permute-start(f32[512,256]{1,0:T(8,128)S(1)} %add.202), channel_id=1, source_target_pairs={{0,1},{1,2},{2,3},{3,0},{4,5},{5,6},{6,7},{7,4},{8,9},{9,10},{10,1... | collective-permute-start | bytes 1572872 | tf_op jit(solution)/shard_map/ppermute | solution.py:104
  117.5 25.5 %collective-permute-start.2 = (f32[512,256]{1,0:T(8,128)S(1)}, f32[512,256]{1,0:T(8,128)S(1)}, u32[]{:S(2)}, u32[]{:S(2)}) collective-permute-start(f32[512,256]{1,0:T(8,128)S(1)} %add.202), channel_id=1, source_target_pairs={{1,0},{2,1},{3,2},{0,3},{5,4},{6,5},{7,6},{4,7},{9,8},{10,9},{11,1... | collective-permute-start | bytes 1572872 | tf_op jit(solution)/shard_map/ppermute | solution.py:106
  131.7 21.3 %copy-start.3 = (f32[512,256]{1,0:T(8,128)}, f32[512,256]{1,0:T(8,128)S(1)}, u32[]{:S(2)}) copy-start(f32[512,256]{1,0:T(8,128)S(1)} %collective-permute-done) | copy-start | bytes 1572868
  131.8 21.3 %collective-permute-start.1 = (f32[512,256]{1,0:T(8,128)S(1)}, f32[512,256]{1,0:T(8,128)S(1)}, u32[]{:S(2)}, u32[]{:S(2)}) collective-permute-start(f32[512,256]{1,0:T(8,128)S(1)} %collective-permute-done), channel_id=1, source_target_pairs={{0,1},{1,2},{2,3},{3,0},{4,5},{5,6},{6,7},{7,4},{8,9},{9,10},{10,1... | collective-permute-start | bytes 1572872 | tf_op jit(solution)/shard_map/ppermute | solution.py:104
  143.0 10.1 %copy-start.4 = (f32[512,256]{1,0:T(8,128)}, f32[512,256]{1,0:T(8,128)S(1)}, u32[]{:S(2)}) copy-start(f32[512,256]{1,0:T(8,128)S(1)} %collective-permute-done.2) | copy-start | bytes 1572868
  153.1 0.8 copy-start.5
  157.5 4.5 copy-start.10
  157.5 4.5 copy-start.11
  189.3 2.0 copy-start.1
  506.6 8.2 copy-start
  517.6 5.2 copy-start.6
  522.9 2.0 copy-start.7
  542.0 2.0 copy-start.1
  859.0 8.2 copy-start
  869.9 5.2 copy-start.6
  875.2 2.0 copy-start.7
  878.5 1.9 copy-start.9
Sparse Core Ops, SparseCore 0:
  27.2 30.6 all-gather.9
  60.0 45.3 all-gather.7
  160.6 11.6 all-gather.5
